TPU v7x, 32 devices: a whole 2x2x4 slice. The times are simulated.
32 devices in a mesh: req: 16 (over z, y, x), tp: 2 (over core).
Axes of the slice: x: 2, y: 2, z: 4, core: 2. Of those that a mesh axis runs over, the one named last changes fastest.
Arguments:
- residual: bfloat16 [512, 2048], P('req'), may hold values from -6 to 6
- fresh_qkv: bfloat16 [512, 3, 2048], P('req', None, 'tp'), may hold values from -32 to 32
- kv_cache: bfloat16 [512, 24, 2, 2048], P('req', None, None, 'tp'), may hold values from -32 to 32
- cache_len: int32 [512], P('req'), may hold values from 2 to 24, as said below
- out_proj: bfloat16 [2048, 2048], P('tp'), may hold values from -0.125 to 0.125
- norm_gain: float32 [2048], replicated, may hold values from 0.1 to 1.9
- router_weight: float32 [2048, 16], replicated, may hold values from -7.9549513 to 7.9549513
- expert_ids: int32 [512, 8], P('req'), may hold values from 0 to 15, all different within a row; in each aligned block of 32 rows (0 to 31, 32 to 63, ...) at most 32 rows name the same one
- gate_up: bfloat16 [16, 2048, 2, 1024], P('req', None, None, 'tp'), may hold values from -0.125 to 0.125
- down_proj: bfloat16 [16, 1024, 2048], P('req', 'tp'), may hold values from -0.1875 to 0.1875
Outputs:
- layer_out: bfloat16 [512, 2048], P('req', 'tp')
Inputs may be any that keep to these rules, and one draw needn't show every extreme that they name: `expert_ids`: each row names 8 different experts; among the 32 rows of one device no expert is named by more than 32 rows, and some device reaches 32. `cache_len`: some request uses all 24 positions.
All inputs are finite; a program needn't handle non-finite values.
Results may differ from a plain program's by a relative error of at most 0.018.
Values may be sent and summed in bfloat16 or wider, within the bound.
A program may use at most 128 MiB of HBM per device.

v0:
```python
import jax
import jax.numpy as jnp
from jax import lax
from jax.sharding import PartitionSpec as P

HD = 128
TOP = 8


def rms_normed(hidden_in, gain):
    values = hidden_in.astype(jnp.float32)
    scale_inv = lax.rsqrt(jnp.mean(values * values, axis=-1, keepdims=True) + 1e-05)
    return (values * scale_inv * gain).astype(jnp.bfloat16)


def expert_part(slots_in, gate_up, down_proj):
    layout = slots_in.shape
    flat_in = slots_in.reshape(-1, layout[-1])
    units_here = down_proj.shape[1]
    both = jnp.dot(
        flat_in, gate_up[0].reshape(layout[-1], 2 * units_here), preferred_element_type=jnp.float32
    )
    both = both.reshape(-1, 2, units_here)
    inner = (jax.nn.silu(both[:, 0]) * both[:, 1]).astype(jnp.bfloat16)
    result = jnp.dot(inner, down_proj[0], preferred_element_type=jnp.float32)
    return result.reshape(layout[:-1] + (down_proj.shape[2],))


def send_back(results):
    return lax.all_to_all(results, "req", split_axis=0, concat_axis=0, tiled=True)


def local(
    residual,
    fresh_qkv,
    kv_cache,
    cache_len,
    out_proj,
    norm_gain,
    router_weight,
    expert_ids,
    gate_up,
    down_proj,
):
    requests = residual.shape[0]
    tp_place = lax.axis_index("tp")
    experts = lax.axis_size("req")
    capacity = 2 * requests * TOP // experts
    local_heads = fresh_qkv.shape[2] // HD
    ctx_len = kv_cache.shape[1]
    queries = fresh_qkv[:, 0].reshape(requests, local_heads, HD)
    new_keys = fresh_qkv[:, 1].reshape(requests, local_heads, HD)
    new_values = fresh_qkv[:, 2].reshape(requests, local_heads, HD)
    cache_keys = kv_cache[:, :, 0].reshape(requests, ctx_len, local_heads, HD)
    cache_values = kv_cache[:, :, 1].reshape(requests, ctx_len, local_heads, HD)
    factor = HD ** (-0.5)
    scores = (
        jnp.einsum("nhd,nchd->nhc", queries, cache_keys, preferred_element_type=jnp.float32)
        * factor
    )
    own_score = (
        jnp.einsum("nhd,nhd->nh", queries, new_keys, preferred_element_type=jnp.float32) * factor
    )
    valid = (jnp.arange(ctx_len, dtype=jnp.int32)[None, :] < cache_len[:, None])[:, None, :]
    masked = jnp.where(valid, scores, -jnp.inf)
    top_score = jnp.maximum(jnp.max(masked, axis=-1), own_score)
    expos = jnp.where(valid, jnp.exp(masked - top_score[..., None]), 0.0)
    own_expo = jnp.exp(own_score - top_score)
    total = jnp.sum(expos, axis=-1) + own_expo
    weights = (expos / total[..., None]).astype(jnp.bfloat16)
    own_weight = (own_expo / total).astype(jnp.bfloat16)
    mixed = jnp.einsum("nhc,nchd->nhd", weights, cache_values, preferred_element_type=jnp.float32)
    mixed = mixed + own_weight.astype(jnp.float32)[..., None] * new_values.astype(jnp.float32)
    attended = mixed.astype(jnp.bfloat16).reshape(requests, local_heads * HD)
    partial_value = jnp.dot(attended, out_proj, preferred_element_type=jnp.float32)
    summed = lax.psum(partial_value, "tp")
    hidden = (residual.astype(jnp.float32) + summed).astype(jnp.bfloat16)
    normed = rms_normed(hidden, norm_gain)
    logits = jnp.dot(normed.astype(jnp.float32), router_weight, precision=lax.Precision.HIGHEST)
    chosen = jnp.take_along_axis(logits, expert_ids, axis=1)
    gate_vals = jax.nn.softmax(chosen, axis=-1)
    flat_ids = expert_ids.reshape(-1)
    onehot = (flat_ids[:, None] == jnp.arange(experts, dtype=jnp.int32)[None, :]).astype(jnp.int32)
    running = jnp.cumsum(onehot, axis=0)
    slot_index = jnp.sum(running * onehot, axis=1) - 1
    position = flat_ids * capacity + slot_index
    selector = (
        position[None, :] == jnp.arange(experts * capacity, dtype=jnp.int32)[:, None]
    ).astype(jnp.float32)
    selector = selector.reshape(experts * capacity, requests, TOP)
    picker = jnp.sum(selector, axis=-1).astype(jnp.bfloat16)
    outgoing = jnp.dot(picker, normed, preferred_element_type=jnp.float32).astype(jnp.bfloat16)
    outgoing = outgoing.reshape(experts, capacity, normed.shape[1])
    combiner = jnp.sum(selector * gate_vals[None, :, :], axis=-1)
    returned = send_back(
        expert_part(
            lax.all_to_all(outgoing, "req", split_axis=0, concat_axis=0, tiled=True),
            gate_up,
            down_proj,
        )
    )
    moe_sum = jnp.dot(
        combiner.T,
        returned.reshape(experts * capacity, -1),
        precision=lax.Precision.HIGHEST,
        preferred_element_type=jnp.float32,
    )
    moe_share = lax.psum_scatter(moe_sum, "tp", scatter_dimension=1, tiled=True)
    width_here = moe_share.shape[1]
    own_cols = lax.dynamic_slice_in_dim(hidden, tp_place * width_here, width_here, 1)
    return (own_cols.astype(jnp.float32) + moe_share).astype(jnp.bfloat16)


def solution(mesh):
    in_specs = (
        P("req", None),
        P("req", None, "tp"),
        P("req", None, None, "tp"),
        P("req"),
        P("tp", None),
        P(),
        P(),
        P("req", None),
        P("req", None, None, "tp"),
        P("req", "tp", None),
    )
    out_specs = P("req", "tp")
    return jax.shard_map(local, mesh=mesh, in_specs=in_specs, out_specs=out_specs, check_vma=False)
```

profile of v0, /device:TPU:0, one launch (start us, length us, event | category | flops | bytes accessed | tf_op | source)
XLA Modules:
  0.0 238.4 jit_solution(5250030907298059460)
XLA Ops:
  6.5 0.0 copy-start
  6.5 0.0 all-reduce.2.cloned.1.call-start
  6.5 1.1 convert_bitcast_fusion
  7.7 0.1 fusion.14
  7.8 0.1 copy.37
  7.8 0.1 reshape.144
  7.9 17.1 %slice_reduce_fusion = (bf16[32,24,1024]{2,1,0:T(8,128)(2,1)}, bf16[32,24,1024]{2,1,0:T(8,128)(2,1)S(1)}) fusion(bf16[32,24,2,1024]{3,2,1,0:T(2,128)(2,1)} %param.12), kind=kLoop, calls=%fused_computation.1 | loop fusion | bytes 6291456 | tf_op jit(solution)/shard_map/slice | solution.py:55
  25.1 0.0 copy-start.5
  25.1 0.9 fusion.5
  26.0 0.1 copy.33
  26.1 0.0 copy-done.5
  26.3 0.2 copy.38
  26.5 0.1 copy.22
  26.5 2.0 fusion.2
  28.5 0.1 fusion.13
  28.7 0.0 copy-start.4
  28.7 0.0 copy-start.1
  28.7 0.0 copy-start.2
  28.7 0.0 copy-start.3
  28.7 3.8 %fusion.18 = f32[32,2048]{1,0:T(8,128)} fusion(bf16[1024,2048]{1,0:T(8,128)(2,1)} %param.14, bf16[4,8,8,128]{3,2,1,0:T(8,128)(2,1)S(1)} %bitcast.109), kind=kOutput, calls=%fused_computation.36 | convolution fusion | flops 134217728 | bytes 4521984 | tf_op jit(solution)/shard_map/dot_general | solution.py:75
  32.5 0.0 all-reduce.2.cloned.1.call-update
  32.5 0.0 copy-done.4
  32.5 0.1 copy.23
  32.6 0.1 eq.39
  32.7 0.1 eq.43
  32.8 0.6 reduce-window.6
  33.4 0.2 slice_reduce_fusion.2
  33.6 0.1 fusion.27
  33.7 0.1 sub.31
  33.8 0.1 reshape.124
  33.9 19.7 %all-reduce.2.cloned.1.call-done = f32[32,2048]{1,0:T(8,128)} async-done(((f32[32,2048]{1,0:T(8,128)}), f32[32,2048]{1,0:T(8,128)}) %all-reduce.2.cloned.1.call-update) | async-done | bytes 262160 | tf_op jit(solution)/shard_map/psum | solution.py:76
  53.6 0.0 copy-done.1
  53.6 1.1 fusion.9
  54.7 0.0 copy-done.2
  54.7 0.0 copy-done.3
  54.8 0.2 fusion.23
  55.0 2.1 gather_fusion
  57.1 0.1 reshape.127
  57.2 0.1 fusion.33
  57.3 0.2 fusion.30
  57.5 0.1 fusion.29
  57.6 0.4 convert_reduce_fusion
  58.0 2.1 convolution_convert_fusion
  60.0 6.8 %all-to-all-start = ((bf16[16,32,2048]{2,1,0:T(8,128)(2,1)}), bf16[16,32,2048]{2,1,0:T(8,128)(2,1)}, u32[]{:S(2)}, u32[]{:S(2)}) async-start(bf16[16,32,2048]{2,1,0:T(8,128)(2,1)} %bitcast.105), calls=%async_computation | async-start | bytes 4194304 | tf_op jit(solution)/shard_map/all_to_all | solution.py:97
  66.9 0.2 reduce-scatter.2.cloned.1.call-start
  67.1 5.3 %copy.49 = bf16[256,8,2,512]{3,1,2,0:T(8,128)(2,1)} copy(bf16[256,8,2,512]{3,2,1,0:T(2,128)(2,1)} %bitcast.106) | data formatting | bytes 8388608
  72.5 6.5 %copy.30 = bf16[1024,2048]{1,0:T(8,128)(2,1)} copy(bf16[1024,2048]{0,1:T(8,128)(2,1)} %bitcast.104) | data formatting | bytes 8388608 | tf_op jit(solution)/shard_map/dot_general | solution.py:20
  78.9 31.2 %all-to-all-done = bf16[16,32,2048]{2,1,0:T(8,128)(2,1)} async-done(((bf16[16,32,2048]{2,1,0:T(8,128)(2,1)}), bf16[16,32,2048]{2,1,0:T(8,128)(2,1)}, u32[]{:S(2)}, u32[]{:S(2)}) %all-to-all-start) | async-done | bytes 2097184 | tf_op jit(solution)/shard_map/all_to_all | solution.py:97
  110.1 5.2 %fusion.34 = f32[512,2,512]{2,0,1:T(8,128)S(1)} fusion(bf16[512,2048,1]{1,0,2:T(8,128)(2,1)} %bitcast.8, bf16[2,512,2048]{2,1,0:T(8,128)(2,1)} %bitcast.107), kind=kOutput, calls=%fused_computation.68 | convolution fusion | flops 2147483648 | bytes 8388608 | tf_op jit(solution)/shard_map/dot_general | solution.py:20
  115.3 0.3 fusion.8
  115.6 0.0 copy-done
  115.7 1.3 fusion
  117.0 103.6 %all_to_all.10 = f32[16,32,2048]{2,1,0:T(8,128)S(1)} all-to-all(f32[16,32,2048]{2,1,0:T(8,128)S(1)} %fusion), channel_id=1, replica_groups=mesh['req'=16,'tp'=2] {'req'}, dimensions={0} | all-to-all | bytes 8388608 | tf_op jit(solution)/shard_map/all_to_all | solution.py:30
  220.5 3.2 %fusion.35 = f32[32,2048]{1,0:T(8,128)} fusion(f32[512,32]{0,1:T(8,128)S(1)} %get-tuple-element.8, f32[512,2048]{1,0:T(8,128)S(1)} %bitcast.103), kind=kOutput, calls=%fused_computation.69 | convolution fusion | flops 402653184 | bytes 4521984 | tf_op jit(solution)/shard_map/dot_general | solution.py:102
  223.7 0.0 reduce-scatter.2.cloned.1.call-update
  223.7 6.3 %reduce-scatter.2.cloned.1.call-done = f32[32,1024]{1,0:T(8,128)} async-done(((f32[32,2048]{1,0:T(8,128)}), f32[32,1024]{1,0:T(8,128)}) %reduce-scatter.2.cloned.1.call-update) | async-done | bytes 131088 | tf_op jit(solution)/shard_map/reduce_scatter | solution.py:108
  230.0 1.6 add_convert_fusion.1
  (16 shorter events, 0.3 us)
Async XLA Ops:
  6.5 109.1 %copy-start = (bf16[1,512,2048]{2,1,0:T(8,128)(2,1)S(1)}, bf16[1,512,2048]{2,1,0:T(8,128)(2,1)}, u32[]{:S(2)}) copy-start(bf16[1,512,2048]{2,1,0:T(8,128)(2,1)} %param.19) | copy-start | bytes 6291460
  6.5 47.1 %all-reduce.2.cloned.1.call-start = ((), (), s32[]{:S(2)}) async-start(), calls=%async_computation.3 | async-start | bytes 524288 | tf_op jit(solution)/shard_map/psum | solution.py:76
  25.1 1.0 copy-start.5
  28.7 3.8 %copy-start.4 = (s32[32,8]{0,1:T(8,128)S(1)}, s32[32,8]{0,1:T(8,128)}, u32[]{:S(2)}) copy-start(s32[32,8]{0,1:T(8,128)} %param.17) | copy-start | bytes 3076
  28.7 25.0 %copy-start.1 = (bf16[32,2048]{1,0:T(8,128)(2,1)S(1)}, bf16[32,2048]{1,0:T(8,128)(2,1)}, u32[]{:S(2)}) copy-start(bf16[32,2048]{1,0:T(8,128)(2,1)} %param.10) | copy-start | bytes 393220
  28.7 26.1 %copy-start.2 = (f32[2048,16]{0,1:T(8,128)S(1)}, f32[2048,16]{0,1:T(8,128)}, u32[]{:S(2)}) copy-start(f32[2048,16]{0,1:T(8,128)} %param.16) | copy-start | bytes 393220
  28.7 26.1 %copy-start.3 = (f32[2048]{0:T(1024)S(1)}, f32[2048]{0:T(1024)}, u32[]{:S(2)}) copy-start(f32[2048]{0:T(1024)} %param.15) | copy-start | bytes 24580
  60.0 50.1 %all-to-all-start = ((bf16[16,32,2048]{2,1,0:T(8,128)(2,1)}), bf16[16,32,2048]{2,1,0:T(8,128)(2,1)}, u32[]{:S(2)}, u32[]{:S(2)}) async-start(bf16[16,32,2048]{2,1,0:T(8,128)(2,1)} %bitcast.105), calls=%async_computation | async-start | bytes 4194304 | tf_op jit(solution)/shard_map/all_to_all | solution.py:97
  66.9 163.1 %reduce-scatter.2.cloned.1.call-start = ((), (), s32[]{:S(2)}) async-start(), calls=%async_computation.4 | async-start | bytes 393216 | tf_op jit(solution)/shard_map/reduce_scatter | solution.py:108
Sparse Core Ops, SparseCore 0:
  32.6 20.9 all-reduce.1
  223.8 6.0 reduce-scatter.1
where the time goes:
time: 239 us; the launch traced here: 238 us
  blocking collectives  104 us (44%)
  waiting for transfers between devices  57.2 us (24%)
  local copies, waits for them, and re-layouts  32.3 us (14%)
  matrix products  18.6 us (8%)
  between operations  13.7 us (6%)
  starting transfers between devices  7.06 us (3%)
  other arithmetic  5.94 us (2%)
    all_to_all x1, blocking collectives, send_back(): lax.all_to_all(results, 'req', split_axis=0, concat_axis=0, tiled=True)  104 us
    all_to_all x1, waiting for transfers between devices, local(): lax.all_to_all(outgoing, 'req', split_axis=0, concat_axis=0, tiled=True)  31.2 us
    psum x1, waiting for transfers between devices, local(): summed = lax.psum(partial_value, 'tp')  19.7 us
    slice x1, local copies, waits for them, and re-layouts, local(): cache_values = kv_cache[:, :, 1].reshape(requests, ctx_len, local_heads, HD)  17.1 us
    all_to_all x1, starting transfers between devices, local(): lax.all_to_all(outgoing, 'req', split_axis=0, concat_axis=0, tiled=True)  6.83 us
    dot_general x1, local copies, waits for them, and re-layouts, expert_part(): jnp.dot(flat_in, gate_up[0].reshape(layout[-1], 2 * units_here), preferre...  6.49 us
    reduce_scatter x1, waiting for transfers between devices, local(): moe_share = lax.psum_scatter(moe_sum, 'tp', scatter_dimension=1, tiled=True)  6.25 us
    unnamed x17, local copies, waits for them, and re-layouts  5.51 us
  transfers between devices with their start and end apart: 3, of which 3 were waited for; matrix products, arithmetic and copies ran while one was open for 6% of the time, Pallas kernels for 0%

commit v1 on v0

v1 whole, which is shorter than its diff:
```python
import jax
import jax.numpy as jnp
from jax import lax
from jax.sharding import PartitionSpec as P

HD = 128


def rms_normed(hidden_in, gain):
    values = hidden_in.astype(jnp.float32)
    scale_inv = lax.rsqrt(jnp.mean(values * values, axis=-1, keepdims=True) + 1e-05)
    return (values * scale_inv * gain).astype(jnp.bfloat16)


def attend(fresh_qkv, kv_cache, cache_len):
    requests, ctx_len = kv_cache.shape[0], kv_cache.shape[1]
    local_heads = fresh_qkv.shape[2] // HD
    queries = fresh_qkv[:, 0].reshape(requests, local_heads, HD)
    new_keys = fresh_qkv[:, 1].reshape(requests, local_heads, HD)
    new_values = fresh_qkv[:, 2].reshape(requests, local_heads, HD)
    cache_keys = kv_cache[:, :, 0].reshape(requests, ctx_len, local_heads, HD)
    cache_values = kv_cache[:, :, 1].reshape(requests, ctx_len, local_heads, HD)
    factor = HD ** (-0.5)
    scores = (
        jnp.einsum("nhd,nchd->nhc", queries, cache_keys, preferred_element_type=jnp.float32)
        * factor
    )
    own_score = (
        jnp.einsum("nhd,nhd->nh", queries, new_keys, preferred_element_type=jnp.float32) * factor
    )
    valid = (jnp.arange(ctx_len, dtype=jnp.int32)[None, :] < cache_len[:, None])[:, None, :]
    masked = jnp.where(valid, scores, -jnp.inf)
    top_score = jnp.maximum(jnp.max(masked, axis=-1), own_score)
    expos = jnp.where(valid, jnp.exp(masked - top_score[..., None]), 0.0)
    own_expo = jnp.exp(own_score - top_score)
    total = jnp.sum(expos, axis=-1) + own_expo
    weights = (expos / total[..., None]).astype(jnp.bfloat16)
    own_weight = (own_expo / total).astype(jnp.bfloat16)
    mixed = jnp.einsum("nhc,nchd->nhd", weights, cache_values, preferred_element_type=jnp.float32)
    mixed = mixed + own_weight.astype(jnp.float32)[..., None] * new_values.astype(jnp.float32)
    return mixed.astype(jnp.bfloat16).reshape(requests, local_heads * HD)


def local(
    residual,
    fresh_qkv,
    kv_cache,
    cache_len,
    out_proj,
    norm_gain,
    router_weight,
    expert_ids,
    gate_up,
    down_proj,
):
    tp_place = lax.axis_index("tp")
    me = lax.axis_index("req")
    experts = lax.axis_size("req")
    attended = attend(fresh_qkv, kv_cache, cache_len)
    partial_value = jnp.dot(attended, out_proj, preferred_element_type=jnp.float32)
    summed = lax.psum(partial_value, "tp")
    hidden = (residual.astype(jnp.float32) + summed).astype(jnp.bfloat16)
    normed = rms_normed(hidden, norm_gain)
    rows = lax.all_gather(normed, "req", axis=0, tiled=True)
    logits = jnp.dot(normed.astype(jnp.float32), router_weight, precision=lax.Precision.HIGHEST)
    named = jnp.any(
        expert_ids[:, :, None] == jnp.arange(experts, dtype=jnp.int32)[None, None, :], axis=1
    )
    gates = jax.nn.softmax(jnp.where(named, logits, -jnp.inf), axis=-1)
    gates_all = lax.all_gather(gates, "req", axis=0, tiled=True)
    mine = jnp.arange(experts, dtype=jnp.int32)[None, :] == me
    weight = jnp.sum(jnp.where(mine, gates_all, 0.0), axis=1, keepdims=True)
    gate_part = jnp.dot(rows, gate_up[0, :, 0], preferred_element_type=jnp.float32)
    up_part = jnp.dot(rows, gate_up[0, :, 1], preferred_element_type=jnp.float32)
    inner = (jax.nn.silu(gate_part) * up_part).astype(jnp.bfloat16)
    result = jnp.dot(inner, down_proj[0], preferred_element_type=jnp.float32)
    own = lax.psum_scatter(result * weight, "tp", scatter_dimension=1, tiled=True)
    moe_share = lax.psum_scatter(own, "req", scatter_dimension=0, tiled=True)
    width_here = moe_share.shape[1]
    own_cols = lax.dynamic_slice_in_dim(hidden, tp_place * width_here, width_here, 1)
    return (own_cols.astype(jnp.float32) + moe_share).astype(jnp.bfloat16)


def solution(mesh):
    in_specs = (
        P("req", None),
        P("req", None, "tp"),
        P("req", None, None, "tp"),
        P("req"),
        P("tp", None),
        P(),
        P(),
        P("req", None),
        P("req", None, None, "tp"),
        P("req", "tp", None),
    )
    out_specs = P("req", "tp")
    return jax.shard_map(local, mesh=mesh, in_specs=in_specs, out_specs=out_specs, check_vma=False)
```

time: 239 us -> 234 us (0.979)
  waiting for transfers between devices: 57.2 us -> 127 us
  blocking collectives: 104 us -> 41.8 us
  starting transfers between devices: 7.06 us -> 0.13 us
  local copies, waits for them, and re-layouts: 32.3 us -> 28.3 us
    all_to_all x1 -> x0, blocking collectives: 104 us -> none  [send_back(): lax.all_to_all(results, 'req', split_axis=0, concat_axis=0, tiled=True)]
    reduce_scatter x1 -> x2, waiting for transfers between devices: 6.25 us -> 94.9 us  [the longest x1 84.1 us: local(): moe_share = lax.psum_scatter(own, 'req', scatter_dimension=0, tiled=True)]
    all_gather x0 -> x1, blocking collectives: none -> 41.8 us  [local(): gates_all = lax.all_gather(gates, 'req', axis=0, tiled=True)]
    all_to_all x1 -> x0, waiting for transfers between devices: 31.2 us -> none  [local(): lax.all_to_all(outgoing, 'req', split_axis=0, concat_axis=0, tiled=True)]
    all_gather x0 -> x1, waiting for transfers between devices: none -> 10.6 us  [local(): rows = lax.all_gather(normed, 'req', axis=0, tiled=True)]
    slice x2, local copies, waits for them, and re-layouts: 17.3 us -> 27.6 us  [the longest x1 17.1 us: attend(): cache_values = kv_cache[:, :, 1].reshape(requests, ctx_len, local_heads, HD)]
    all_to_all x1 -> x0, starting transfers between devices: 6.83 us -> none  [local(): lax.all_to_all(outgoing, 'req', split_axis=0, concat_axis=0, tiled=True)]
    dot_general x3 -> x2, local copies, waits for them, and re-layouts: 6.67 us -> 0.18 us  [the longest x1 0.12 us: attend(): jnp.einsum('nhd,nchd->nhc', queries, cache_keys, preferred_element_type=j...]
  transfers between devices with their start and end apart: 3 -> 4, of which waited for: 3 -> 4; matrix products, arithmetic and copies ran while one was open for 6% -> 5% of each run, Pallas kernels for 0% -> 0%
where the time goes in v1:
time: 234 us
  waiting for transfers between devices  127 us (54%)
  blocking collectives  41.8 us (18%)
  local copies, waits for them, and re-layouts  28.3 us (12%)
  matrix products  18.2 us (8%)
  between operations  13.3 us (6%)
  other arithmetic  5.64 us (2%)
    reduce_scatter x1, waiting for transfers between devices, local(): moe_share = lax.psum_scatter(own, 'req', scatter_dimension=0, tiled=True)  84.1 us
    all_gather x1, blocking collectives, local(): gates_all = lax.all_gather(gates, 'req', axis=0, tiled=True)  41.8 us
    psum x1, waiting for transfers between devices, local(): summed = lax.psum(partial_value, 'tp')  21.1 us
    slice x1, local copies, waits for them, and re-layouts, attend(): cache_values = kv_cache[:, :, 1].reshape(requests, ctx_len, local_heads, HD)  17.1 us
    reduce_scatter x1, waiting for transfers between devices, local(): lax.psum_scatter(result * weight, 'tp', scatter_dimension=1, tiled=True)  10.8 us
    all_gather x1, waiting for transfers between devices, local(): rows = lax.all_gather(normed, 'req', axis=0, tiled=True)  10.6 us
    slice x1, local copies, waits for them, and re-layouts, local(): gate_up[0, :, 0]  10.4 us
    dot_general x1, matrix products, local(): result = jnp.dot(inner, down_proj[0], preferred_element_type=jnp.float32)  7.25 us
  transfers between devices with their start and end apart: 4, of which 4 were waited for; matrix products, arithmetic and copies ran while one was open for 5% of the time, Pallas kernels for 0%

profile of v1, /device:TPU:0, one launch (start us, length us, event | category | flops | bytes accessed | tf_op | source)
XLA Modules:
  0.0 234.0 jit_solution(13227113264910571109)
XLA Ops:
  6.5 0.0 copy-start
  6.5 0.0 all-reduce.2.cloned.1.call-start
  6.5 0.8 iota_compare_fusion.1
  7.4 0.9 convert_bitcast_fusion
  8.4 0.1 fusion.20
  8.5 0.1 copy.30
  8.5 0.1 reshape.54
  8.6 17.1 %slice_reduce_fusion = (bf16[32,24,1024]{2,1,0:T(8,128)(2,1)}, bf16[32,24,1024]{2,1,0:T(8,128)(2,1)S(1)}) fusion(bf16[32,24,2,1024]{3,2,1,0:T(2,128)(2,1)} %param.12), kind=kLoop, calls=%fused_computation.1 | loop fusion | bytes 6291456 | tf_op jit(solution)/shard_map/slice | solution.py:22
  25.7 0.9 fusion.6
  26.7 0.1 copy.26
  26.9 0.1 copy.20
  27.0 0.2 copy.31
  27.2 2.0 fusion.3
  29.2 0.1 fusion.19
  29.3 0.0 copy-start.2
  29.3 0.0 copy-start.4
  29.3 0.0 copy-start.5
  29.3 3.8 %fusion.24 = f32[32,2048]{1,0:T(8,128)} fusion(bf16[1024,2048]{1,0:T(8,128)(2,1)} %param.14, bf16[4,8,8,128]{3,2,1,0:T(8,128)(2,1)S(1)} %bitcast.84), kind=kOutput, calls=%fused_computation.40 | convolution fusion | flops 134217728 | bytes 4521984 | tf_op jit(solution)/shard_map/dot_general | solution.py:60
  33.1 0.0 all-reduce.2.cloned.1.call-update
  33.1 0.0 all-gather.3.cloned.1.call-start
  33.2 21.1 %all-reduce.2.cloned.1.call-done = f32[32,2048]{1,0:T(8,128)} async-done(((f32[32,2048]{1,0:T(8,128)}), f32[32,2048]{1,0:T(8,128)}) %all-reduce.2.cloned.1.call-update) | async-done | bytes 262160 | tf_op jit(solution)/shard_map/psum | solution.py:61
  54.3 0.0 copy-done.2
  54.3 1.1 fusion.15
  55.4 0.0 copy-done.4
  55.4 0.7 fusion.17
  56.1 0.0 all-gather.3.cloned.1.call-update
  56.1 0.0 reduce-scatter.3.cloned.1.call-start
  56.2 0.0 copy-done.5
  56.2 0.0 copy-start.1
  56.3 0.0 copy-start.3
  56.3 10.4 %fusion.33 = (bf16[1,2048,1,512]{3,2,1,0:T(2,128)(2,1)}, bf16[1,2048,1,512]{3,2,1,0:T(2,128)(2,1)}) fusion(bf16[1,2048,2,512]{3,2,1,0:T(2,128)(2,1)} %param.18), kind=kLoop, calls=%fused_computation.61 | loop fusion | bytes 8388608 | tf_op jit(solution)/shard_map/slice | solution.py:73
  66.7 0.0 copy-done.1
  66.7 0.0 copy-done.3
  66.7 0.2 fusion.34
  67.0 41.8 %all-gather = f32[16,32,16]{1,2,0:T(8,128)S(1)} all-gather(f32[1,32,16]{1,2,0:T(8,128)S(1)} %divide_bitcast_fusion), channel_id=1, replica_groups=mesh['req'=16,'tp'=2] {'req'}, dimensions={0}, use_global_device_ids=true | all-gather | bytes 34816 | tf_op jit(solution)/shard_map/all_gather | solution.py:70
  108.9 0.1 reshape.46
  109.0 0.1 select_reduce_fusion
  109.1 10.6 %all-gather.3.cloned.1.call-done = bf16[512,2048]{1,0:T(8,128)(2,1)} async-done(((bf16[32,2048]{1,0:T(8,128)(2,1)}), bf16[512,2048]{1,0:T(8,128)(2,1)}) %all-gather.3.cloned.1.call-update) | async-done | bytes 2097168 | tf_op jit(solution)/shard_map/all_gather | solution.py:64
  119.6 4.1 %fusion.1 = f32[512,512]{1,0:T(8,128)S(1)} fusion(bf16[512,2048]{1,0:T(8,128)(2,1)} %all-gather.3.cloned.1.call-done, bf16[1,2048,1,512]{3,2,1,0:T(2,128)(2,1)} %get-tuple-element.9), kind=kOutput, calls=%fused_computation.6 | convolution fusion | flops 1073741824 | bytes 5242880 | tf_op jit(solution)/shard_map/dot_general | solution.py:73
  123.7 0.0 copy-done
  123.7 7.3 %convolution_multiply_fusion = f32[512,2048]{1,0:T(8,128)} fusion(bf16[1,512,2048]{2,1,0:T(8,128)(2,1)S(1)} %copy-done, f32[512]{0:T(512)S(1)} %select_reduce_fusion, bf16[512,2048]{1,0:T(8,128)(2,1)} %all-gather.3.cloned.1.call-done, bf16[1,2048,1,512]{3,2,1,0:T(2,128)(2,1)} %get-tuple-element.10, f32[512,512]{1,0:T(8,128)S(1)} %fusion.1), kind=kOutput, calls=%fused_computation | convolution fusion | flops 2150105088 | bytes 11536384 | tf_op jit(solution)/shard_map/dot_general | solution.py:76
  131.0 0.0 reduce-scatter.3.cloned.1.call-update
  131.0 0.0 reduce-scatter.5.cloned.1.call-start
  131.1 10.8 %reduce-scatter.3.cloned.1.call-done = f32[512,1024]{1,0:T(8,128)} async-done(((f32[512,2048]{1,0:T(8,128)}), f32[512,1024]{1,0:T(8,128)}) %reduce-scatter.3.cloned.1.call-update) | async-done | bytes 2097168 | tf_op jit(solution)/shard_map/reduce_scatter | solution.py:77
  141.8 0.0 reduce-scatter.5.cloned.1.call-update
  141.9 84.1 %reduce-scatter.5.cloned.1.call-done = f32[32,1024]{1,0:T(8,128)} async-done(((f32[512,1024]{1,0:T(8,128)}), f32[32,1024]{1,0:T(8,128)}) %reduce-scatter.5.cloned.1.call-update) | async-done | bytes 131088 | tf_op jit(solution)/shard_map/reduce_scatter | solution.py:78
  226.0 1.5 add_convert_fusion.1
  (14 shorter events, 0.3 us)
Async XLA Ops:
  6.5 117.2 %copy-start = (bf16[1,512,2048]{2,1,0:T(8,128)(2,1)S(1)}, bf16[1,512,2048]{2,1,0:T(8,128)(2,1)}, u32[]{:S(2)}) copy-start(bf16[1,512,2048]{2,1,0:T(8,128)(2,1)} %param.19) | copy-start | bytes 6291460
  6.5 47.7 %all-reduce.2.cloned.1.call-start = ((), (), s32[]{:S(2)}) async-start(), calls=%async_computation.2 | async-start | bytes 524288 | tf_op jit(solution)/shard_map/psum | solution.py:61
  29.3 25.0 %copy-start.2 = (bf16[32,2048]{1,0:T(8,128)(2,1)S(1)}, bf16[32,2048]{1,0:T(8,128)(2,1)}, u32[]{:S(2)}) copy-start(bf16[32,2048]{1,0:T(8,128)(2,1)} %param.10) | copy-start | bytes 393220
  29.3 26.1 %copy-start.4 = (f32[2048]{0:T(1024)S(1)}, f32[2048]{0:T(1024)}, u32[]{:S(2)}) copy-start(f32[2048]{0:T(1024)} %param.15) | copy-start | bytes 24580
  29.3 26.9 %copy-start.5 = (s32[32,8]{0,1:T(8,128)S(1)}, s32[32,8]{0,1:T(8,128)}, u32[]{:S(2)}) copy-start(s32[32,8]{0,1:T(8,128)} %param.17) | copy-start | bytes 3076
  33.1 86.5 %all-gather.3.cloned.1.call-start = ((), (), s32[]{:S(2)}) async-start(), calls=%async_computation.3 | async-start | bytes 2228224 | tf_op jit(solution)/shard_map/all_gather | solution.py:64
  56.1 85.7 %reduce-scatter.3.cloned.1.call-start = ((), (), s32[]{:S(2)}) async-start(), calls=%async_computation.4 | async-start | bytes 6291456 | tf_op jit(solution)/shard_map/reduce_scatter | solution.py:77
  56.2 10.5 %copy-start.1 = (bf16[32,2048]{1,0:T(8,128)(2,1)S(1)}, bf16[32,2048]{1,0:T(8,128)(2,1)}, u32[]{:S(2)}) copy-start(bf16[32,2048]{1,0:T(8,128)(2,1)} %fusion.17) | copy-start | bytes 393220
  56.3 10.5 %copy-start.3 = (f32[2048,16]{0,1:T(8,128)S(1)}, f32[2048,16]{0,1:T(8,128)}, u32[]{:S(2)}) copy-start(f32[2048,16]{0,1:T(8,128)} %param.16) | copy-start | bytes 393220
  131.0 95.0 %reduce-scatter.5.cloned.1.call-start = ((), (), s32[]{:S(2)}) async-start(), calls=%async_computation.5 | async-start | bytes 2228224 | tf_op jit(solution)/shard_map/reduce_scatter | solution.py:78
Sparse Core Ops, SparseCore 0:
  33.3 20.9 all-reduce.1
  57.4 62.1 all-gather.2
  131.1 10.6 reduce-scatter.2
  144.0 81.9 reduce-scatter.4

commit v2 on v1

v2 whole, which is shorter than its diff:
```python
import functools

import jax
import jax.numpy as jnp
from jax import lax
from jax.experimental import pallas as pl
from jax.experimental.pallas import tpu as pltpu
from jax.sharding import PartitionSpec as P

HD = 128


def attend(fresh_qkv, kv_cache, cache_len):
    requests, ctx_len = kv_cache.shape[0], kv_cache.shape[1]
    local_heads = fresh_qkv.shape[2] // HD
    queries = fresh_qkv[:, 0].reshape(requests, local_heads, HD)
    new_keys = fresh_qkv[:, 1].reshape(requests, local_heads, HD)
    new_values = fresh_qkv[:, 2].reshape(requests, local_heads, HD)
    cache_keys = kv_cache[:, :, 0].reshape(requests, ctx_len, local_heads, HD)
    cache_values = kv_cache[:, :, 1].reshape(requests, ctx_len, local_heads, HD)
    factor = HD ** (-0.5)
    scores = (
        jnp.einsum("nhd,nchd->nhc", queries, cache_keys, preferred_element_type=jnp.float32)
        * factor
    )
    own_score = (
        jnp.einsum("nhd,nhd->nh", queries, new_keys, preferred_element_type=jnp.float32) * factor
    )
    valid = (jnp.arange(ctx_len, dtype=jnp.int32)[None, :] < cache_len[:, None])[:, None, :]
    masked = jnp.where(valid, scores, -jnp.inf)
    top_score = jnp.maximum(jnp.max(masked, axis=-1), own_score)
    expos = jnp.where(valid, jnp.exp(masked - top_score[..., None]), 0.0)
    own_expo = jnp.exp(own_score - top_score)
    total = jnp.sum(expos, axis=-1) + own_expo
    weights = (expos / total[..., None]).astype(jnp.bfloat16)
    own_weight = (own_expo / total).astype(jnp.bfloat16)
    mixed = jnp.einsum("nhc,nchd->nhd", weights, cache_values, preferred_element_type=jnp.float32)
    mixed = mixed + own_weight.astype(jnp.float32)[..., None] * new_values.astype(jnp.float32)
    return mixed.astype(jnp.bfloat16).reshape(requests, local_heads * HD)


def moe_kernel(
    deep,
    plane,
    cores,
    partial,
    residual,
    gain,
    router,
    named,
    gate_hbm,
    up_hbm,
    down_hbm,
    out,
    parts,
    hidden,
    normed,
    gathered,
    gate_w,
    up_w,
    down_w,
    core_out,
    core_in,
    plane_out,
    plane_in,
    deep_out,
    deep_in,
    load_sem,
    parts_send,
    parts_recv,
    own_send,
    pass_send,
    slot_recv,
    cross_send,
    cross_recv,
    core_send,
    core_recv,
    plane_send,
    plane_recv,
    deep_send,
    deep_recv,
):
    me = lax.axis_index("req")
    core = lax.axis_index("tp")
    level = me // plane
    place = lax.rem(me, plane)
    tokens, width = residual.shape
    cols = width // cores
    f32, bf16 = jnp.float32, jnp.bfloat16

    loads = [
        pltpu.make_async_copy(src, dst, load_sem.at[i])
        for i, (src, dst) in enumerate(((gate_hbm, gate_w), (up_hbm, up_w), (down_hbm, down_w)))
    ]
    for load in loads:
        load.start()

    def core_at(i):
        return lax.rem(core + i, cores)

    def level_at(i):
        return lax.rem(level + i, deep)

    def place_at(i):
        return lax.rem(place + i, plane)

    barrier = pltpu.get_barrier_semaphore()
    greeted = [(me, core_at(i)) for i in range(1, cores)]
    greeted += [(level_at(i) * plane + place, core) for i in range(1, deep)]
    greeted += [(level * plane + place_at(i), core) for i in range(1, plane)]
    for device in greeted:
        pl.semaphore_signal(barrier, inc=1, device_id=device, device_id_type=pl.DeviceIdType.MESH)
    pl.semaphore_wait(barrier, len(greeted))

    def send(src, dst, send_sem, recv_sem, device):
        copy = pltpu.make_async_remote_copy(
            src_ref=src,
            dst_ref=dst,
            send_sem=send_sem,
            recv_sem=recv_sem,
            device_id=device,
            device_id_type=pl.DeviceIdType.MESH,
        )
        copy.start()
        started.append(copy)

    def arrived(dst, recv_sem):
        pltpu.make_async_copy(dst, dst, recv_sem).wait()

    started = []
    for i in range(1, cores):
        send(partial, parts.at[i - 1], parts_send.at[i - 1], parts_recv.at[i - 1], (me, core_at(i)))
    for i in range(1, cores):
        arrived(parts.at[i - 1], parts_recv.at[i - 1])
    summed = partial[...]
    for i in range(1, cores):
        summed = summed + parts[i - 1]
    hidden[...] = (residual[...].astype(f32) + summed).astype(bf16)
    values = hidden[...].astype(f32)
    scale_inv = lax.rsqrt(jnp.mean(values * values, axis=-1, keepdims=True) + 1e-05)
    normed[...] = (values * scale_inv * gain[...]).astype(bf16)
    logits = jnp.dot(
        normed[...].astype(f32),
        router[...],
        precision=lax.Precision.HIGHEST,
        preferred_element_type=f32,
    )
    half = router.shape[1] // 2
    lane = lax.broadcasted_iota(jnp.int32, logits.shape, 1)
    chosen = named[...] > 0.0
    top = jnp.max(jnp.where(chosen, logits, -jnp.inf), axis=1, keepdims=True)
    expos = jnp.where(chosen, jnp.exp(jnp.where(chosen, logits, top) - top), 0.0)
    total = jnp.sum(jnp.where(lane < half, expos, 0.0), axis=1, keepdims=True)
    gates = expos / total
    high = gates.astype(bf16).astype(f32)
    own_cols = pl.ds(pl.multiple_of(core * cols, 128), cols)
    gathered[core, me, :, 0:cols] = normed[:, own_cols]
    gathered[core, me, :, cols:] = jnp.where(lane < half, high, gates - high).astype(bf16)

    def spread(k):
        slot = level_at(deep - k) * plane + place if k else me
        block = gathered.at[core, slot]
        for j in range(1, plane):
            send(
                block,
                block,
                pass_send.at[k, j - 1],
                slot_recv.at[slot],
                (level * plane + place_at(j), core),
            )

    def cross(k, j):
        slot = level_at(deep - k) * plane + place_at(j)
        block = gathered.at[core, slot]
        for i in range(1, cores):
            send(
                block,
                block,
                cross_send.at[k, j, i - 1],
                cross_recv.at[i - 1, slot],
                (me, core_at(i)),
            )

    mine = gathered.at[core, me]
    for i in range(1, deep):
        send(mine, mine, own_send.at[i - 1], slot_recv.at[me], (level_at(i) * plane + place, core))
    spread(0)
    cross(0, 0)
    for k in range(1, deep):
        slot = level_at(deep - k) * plane + place
        arrived(gathered.at[core, slot], slot_recv.at[slot])
        spread(k)
        cross(k, 0)

    def collect(k):
        first = level_at(deep - k) * plane
        for j in range(1, plane):
            slot = first + place_at(j)
            arrived(gathered.at[core, slot], slot_recv.at[slot])
            cross(k, j)
        for i in range(1, cores):
            for j in range(plane):
                slot = first + place_at(j)
                arrived(gathered.at[core_at(cores - i), slot], cross_recv.at[i - 1, slot])

    def work(k):
        slots = pl.ds(level_at(deep - k) * plane, plane)
        gate_part = up_part = 0.0
        for t in range(cores):
            block = gathered[t, slots, :, 0:cols].reshape(plane * tokens, cols)
            span = slice(t * cols, (t + 1) * cols)
            gate_part += jnp.dot(block, gate_w[span, :], preferred_element_type=f32)
            up_part += jnp.dot(block, up_w[span, :], preferred_element_type=f32)
        inner = (gate_part * (1.0 / (1.0 + jnp.exp(-gate_part))) * up_part).astype(bf16)
        extra = gathered[0, slots, :, cols:].reshape(plane * tokens, 2 * half).astype(f32)
        spot = lax.broadcasted_iota(jnp.int32, extra.shape, 1)
        weight = jnp.sum(
            jnp.where((spot == me) | (spot == me + half), extra, 0.0), axis=1, keepdims=True
        )
        for i in range(1, cores + 1):
            span = pl.ds(pl.multiple_of(core_at(i) * cols, 128), cols)
            result = jnp.dot(inner, down_w[:, span], preferred_element_type=f32) * weight
            core_out[k, i - 1] = result.astype(core_out.dtype).reshape(plane, tokens, cols)
            if i < cores:
                send(
                    core_out.at[k, i - 1],
                    core_in.at[k, i - 1],
                    core_send.at[k, i - 1],
                    core_recv.at[k, i - 1],
                    (me, core_at(i)),
                )

    def over_plane(k):
        for i in range(1, cores):
            arrived(core_in.at[k, i - 1], core_recv.at[k, i - 1])
        for j in list(range(1, plane)) + [0]:
            whole = core_out[k, cores - 1, place_at(j)].astype(f32)
            for i in range(1, cores):
                whole = whole + core_in[k, i - 1, place_at(j)].astype(f32)
            plane_out[k, j] = whole.astype(bf16)
            if j:
                send(
                    plane_out.at[k, j],
                    plane_in.at[k, j - 1],
                    plane_send.at[k, j - 1],
                    plane_recv.at[k, j - 1],
                    (level * plane + place_at(j), core),
                )

    def over_deep(k):
        whole = plane_out[k, 0].astype(f32)
        for j in range(1, plane):
            arrived(plane_in.at[k, j - 1], plane_recv.at[k, j - 1])
            whole = whole + plane_in[k, j - 1].astype(f32)
        if k:
            deep_out[k - 1] = whole.astype(bf16)
            send(
                deep_out.at[k - 1],
                deep_in.at[k - 1],
                deep_send.at[k - 1],
                deep_recv.at[k - 1],
                (level_at(deep - k) * plane + place, core),
            )
        return whole

    own_sum = None
    for step in range(deep + 2):
        if step < deep:
            collect(step)
            if step == 0:
                for load in loads:
                    load.wait()
            work(step)
        if 1 <= step <= deep:
            over_plane(step - 1)
        if step >= 2:
            found = over_deep(step - 2)
            own_sum = found if step == 2 else own_sum
    for k in range(1, deep):
        arrived(deep_in.at[k - 1], deep_recv.at[k - 1])
        own_sum = own_sum + deep_in[k - 1].astype(f32)
    out[...] = (hidden[:, own_cols].astype(f32) + own_sum).astype(bf16)
    for copy in started:
        copy.wait_send()


def moe_call(partial, residual, gain, router, named, gate_w, up_w, down_w):
    shards, cores = lax.axis_size("req"), lax.axis_size("tp")
    deep = 4
    plane = shards // deep
    tokens, width = residual.shape
    units = down_w.shape[0]
    cols = width // cores
    bf16, dma = jnp.bfloat16, pltpu.SemaphoreType.DMA
    others = cores - 1
    vmem = pl.BlockSpec(memory_space=pltpu.VMEM)
    hbm = pl.BlockSpec(memory_space=pl.ANY)
    return pl.pallas_call(
        functools.partial(moe_kernel, deep, plane, cores),
        out_shape=jax.ShapeDtypeStruct((tokens, cols), bf16),
        in_specs=[vmem] * 5 + [hbm] * 3,
        out_specs=vmem,
        scratch_shapes=[
            pltpu.VMEM((others, tokens, width), jnp.float32),
            pltpu.VMEM((tokens, width), bf16),
            pltpu.VMEM((tokens, width), bf16),
            pltpu.VMEM((cores, shards, tokens, cols + router.shape[1]), bf16),
            pltpu.VMEM((width, units), bf16),
            pltpu.VMEM((width, units), bf16),
            pltpu.VMEM((units, width), bf16),
            pltpu.VMEM((deep, cores, plane, tokens, cols), bf16),
            pltpu.VMEM((deep, others, plane, tokens, cols), bf16),
            pltpu.VMEM((deep, plane, tokens, cols), bf16),
            pltpu.VMEM((deep, plane - 1, tokens, cols), bf16),
            pltpu.VMEM((deep - 1, tokens, cols), bf16),
            pltpu.VMEM((deep - 1, tokens, cols), bf16),
            dma((3,)),
            dma((others,)),
            dma((others,)),
            dma((deep - 1,)),
            dma((deep, plane - 1)),
            dma((shards,)),
            dma((deep, plane, others)),
            dma((others, shards)),
            dma((deep, others)),
            dma((deep, others)),
            dma((deep, plane - 1)),
            dma((deep, plane - 1)),
            dma((deep - 1,)),
            dma((deep - 1,)),
        ],
        compiler_params=pltpu.CompilerParams(
            collective_id=0, has_side_effects=True, vmem_limit_bytes=56 * 1024 * 1024
        ),
    )(partial, residual, gain, router, named, gate_w, up_w, down_w)


def local(
    residual,
    fresh_qkv,
    kv_cache,
    cache_len,
    out_proj,
    norm_gain,
    router_weight,
    expert_ids,
    gate_up,
    down_proj,
):
    experts = lax.axis_size("req")
    attended = attend(fresh_qkv, kv_cache, cache_len)
    partial_value = jnp.dot(attended, out_proj, preferred_element_type=jnp.float32)
    half = 64 * (-(-experts // 64))
    lanes = lax.rem(jnp.arange(2 * half, dtype=jnp.int32), half)
    named = jnp.any(expert_ids[:, :, None] == lanes[None, None, :], axis=1).astype(jnp.float32)
    router = jnp.pad(router_weight, ((0, 0), (0, half - experts)))
    router = jnp.concatenate([router, router], axis=1)
    return moe_call(
        partial_value,
        residual,
        norm_gain[None, :],
        router,
        named,
        gate_up[0, :, 0],
        gate_up[0, :, 1],
        down_proj[0],
    )


def solution(mesh):
    in_specs = (
        P("req", None),
        P("req", None, "tp"),
        P("req", None, None, "tp"),
        P("req"),
        P("tp", None),
        P(),
        P(),
        P("req", None),
        P("req", None, None, "tp"),
        P("req", "tp", None),
    )
    out_specs = P("req", "tp")
    return jax.shard_map(local, mesh=mesh, in_specs=in_specs, out_specs=out_specs, check_vma=False)
```

time: 234 us -> 82.3 us (0.35)
  waiting for transfers between devices: 127 us -> 0 us
  Pallas kernels: 0 us -> 45.3 us
  blocking collectives: 41.8 us -> 0 us
  between operations: 13.3 us -> 0.18 us
  matrix products: 18.2 us -> 5.37 us
    reduce_scatter x2 -> x0, waiting for transfers between devices: 94.9 us -> none  [the longest x1 84.1 us: local(): moe_share = lax.psum_scatter(own, 'req', scatter_dimension=0, tiled=True)]
    pallas_call x0 -> x1, Pallas kernels: none -> 45.3 us  [moe_call(): pl.pallas_call(functools.partial(moe_kernel, deep, plane, cores), out_sha...]
    all_gather x1 -> x0, blocking collectives: 41.8 us -> none  [local(): gates_all = lax.all_gather(gates, 'req', axis=0, tiled=True)]
    psum x1 -> x0, waiting for transfers between devices: 21.1 us -> none  [local(): summed = lax.psum(partial_value, 'tp')]
    dot_general x3 -> x0, matrix products: 11.6 us -> none  [the longest x1 7.25 us: local(): result = jnp.dot(inner, down_proj[0], preferred_element_type=jnp.float32)]
    all_gather x1 -> x0, waiting for transfers between devices: 10.6 us -> none  [local(): rows = lax.all_gather(normed, 'req', axis=0, tiled=True)]
    slice x1, local copies, waits for them, and re-layouts: 10.4 us -> 6.1 us  [local(): gate_up[0, :, 1]]
    squeeze x0 -> x1, local copies, waits for them, and re-layouts: none -> 3.16 us  [local(): gate_up[0, :, 1]]
  transfers between devices with their start and end apart: 4 -> 0, of which waited for: 4 -> 0; matrix products, arithmetic and copies ran while one was open for 5% -> 0% of each run, Pallas kernels for 0% -> 0%
where the time goes in v2:
time: 82.3 us; the launch traced here: 82 us
  Pallas kernels  45.3 us (55%)
  local copies, waits for them, and re-layouts  27.9 us (34%)
  matrix products  5.37 us (7%)
  other arithmetic  3.33 us (4%)
    pallas_call x1, Pallas kernels, moe_call(): pl.pallas_call(functools.partial(moe_kernel, deep, plane, cores), out_sha...  45.3 us
    slice x1, local copies, waits for them, and re-layouts, attend(): cache_values = kv_cache[:, :, 1].reshape(requests, ctx_len, local_heads, HD)  16.1 us
    slice x1, local copies, waits for them, and re-layouts, local(): gate_up[0, :, 1]  6.1 us
    dot_general x1, matrix products, local(): jnp.dot(attended, out_proj, preferred_element_type=jnp.float32)  3.88 us
    squeeze x1, local copies, waits for them, and re-layouts, local(): gate_up[0, :, 1]  3.16 us
    unnamed x14, local copies, waits for them, and re-layouts  1.97 us

profile of v2, /device:TPU:0, one launch (start us, length us, event | category | flops | bytes accessed | tf_op | source)
XLA Modules:
  0.0 82.0 jit_solution(14935392330321473909)
XLA Ops:
  0.0 0.9 %convert_bitcast_fusion = (f32[4,8,8,128]{3,1,2,0:T(8,128)S(1)}, bf16[4,8,8,128]{3,1,2,0:T(8,128)(2,1)S(1)}, bf16[32,1,1024]{2,0,1:T(8,128)(2,1)S(1)}, bf16[4,8,8,128]{3,1,2,0:T(8,128)(2,1)S(1)}) fusion(bf16[32,3,1024]{2,0,1:T(8,128)(2,1)} %param.11), kind=kLoop, calls=%fused_computation.16 | loop fusion | flops 32768 | bytes 524288
  0.9 0.1 reshape.39
  1.0 16.1 %slice_reduce_fusion = (bf16[32,24,1024]{2,1,0:T(8,128)(2,1)S(1)}, bf16[32,24,1024]{2,1,0:T(8,128)(2,1)S(1)}) fusion(bf16[32,24,2,1024]{3,2,1,0:T(2,128)(2,1)} %param.12), kind=kLoop, calls=%fused_computation | loop fusion | bytes 6291456 | tf_op jit(solution)/shard_map/slice | solution.py:20
  17.1 0.0 copy-start.3
  17.1 0.9 %fusion.3 = f32[32,8,1,24]{3,2,1,0:T(1,128)S(1)} fusion(bf16[32,8,128,1]{2,3,1,0:T(2,128)(2,1)S(1)} %reshape.39, bf16[32,24,1024]{2,1,0:T(8,128)(2,1)S(1)} %get-tuple-element.6), kind=kOutput, calls=%fused_computation.7 | convolution fusion | flops 1572864 | bytes 1662976 | tf_op jit(solution)/shard_map/nhd,nchd->nhc/dot_general | solution.py:23
  18.0 0.1 copy.26
  18.2 0.0 copy-done.3
  18.3 0.1 fusion.8
  18.4 0.1 copy.30
  18.6 0.2 copy.31
  18.7 0.6 fusion
  19.3 0.1 copy.19
  19.4 0.1 fusion.7
  19.5 0.0 copy-start
  19.6 3.9 %fusion.12.partial = f32[32,2048]{1,0:T(8,128)} fusion(bf16[1024,2048]{1,0:T(8,128)(2,1)} %param.14, bf16[4,8,8,128]{3,2,1,0:T(8,128)(2,1)S(1)} %bitcast.68), kind=kOutput, calls=%fused_computation.24 | convolution fusion | flops 134217728 | bytes 4521984 | tf_op jit(solution)/shard_map/dot_general | solution.py:352
  23.4 0.0 copy-done
  23.4 6.1 %fusion.18 = (bf16[1,2048,1,512]{3,2,1,0:T(2,128)(2,1)S(1)}, bf16[1,2048,1,512]{3,2,1,0:T(2,128)(2,1)S(1)}) fusion(bf16[1,2048,2,512]{3,2,1,0:T(2,128)(2,1)S(1)} %copy-done), kind=kLoop, calls=%fused_computation.37 | loop fusion | bytes 8388608 | tf_op jit(solution)/shard_map/slice | solution.py:365
  29.5 0.0 copy-start.1
  29.6 3.2 %copy_bitcast_fusion = (bf16[2048,512]{1,0:T(8,128)(2,1)}, bf16[2048,512]{1,0:T(8,128)(2,1)}) fusion(bf16[1,2048,1,512]{3,2,1,0:T(2,128)(2,1)S(1)} %get-tuple-element.7, bf16[1,2048,1,512]{3,2,1,0:T(2,128)(2,1)S(1)} %get-tuple-element.8), kind=kLoop, calls=%fused_computation.2 | loop fusion | bytes 8388608 | tf_op jit(solution)/shard_map/squeeze | solution.py:365
  32.7 0.0 copy-done.1
  32.7 0.3 copy.20
  33.1 0.0 copy-start.2
  33.1 0.1 pad.4
  33.1 1.3 %pad_maximum_fusion.router = f32[2048,128]{1,0:T(8,128)} fusion(f32[2048,64]{1,0:T(8,128)S(1)} %pad.4), kind=kLoop, calls=%fused_computation.10 | loop fusion | flops 262144 | bytes 1572864 | tf_op jit(solution)/shard_map/concatenate | solution.py:357
  34.5 0.0 copy-done.2
  34.5 0.1 copy.21
  34.5 0.1 compare_reduce_fusion
  34.7 0.6 convert_element_type.29.named
  35.3 45.3 %shard_map.100 = bf16[32,1024]{1,0:T(8,128)(2,1)} custom-call(f32[32,2048]{1,0:T(8,128)} %fusion.12.partial, bf16[32,2048]{1,0:T(8,128)(2,1)} %residual.1, f32[1,2048]{1,0:T(1,128)} %bitcast.72, f32[2048,128]{1,0:T(8,128)} %pad_maximum_fusion.router, f32[32,128]{1,0:T(8,128)} %convert_element_type.29.named, bf16[2048,512]{1,0:T(8,128)(2,1)} %get-tuple-element.16.gate_hbm, ...), custom_call_target="tpu_custom_call" | custom-call | tf_op jit(solution)/shard_map/pallas_call | solution.py:298
  80.6 1.5 %copy.58 = bf16[32,1024]{1,0:T(8,128)(2,1)} copy(bf16[32,1024]{1,0:T(8,128)(2,1)} %shard_map.100) | data formatting | bytes 131072
  (10 shorter events, 0.2 us)
Async XLA Ops:
  17.1 1.0 %copy-start.3 = (s32[32]{0:T(128)S(1)}, s32[32]{0:T(128)}, u32[]{:S(2)}) copy-start(s32[32]{0:T(128)} %param.13) | copy-start | bytes 388
  19.5 3.9 %copy-start = (bf16[1,2048,2,512]{3,2,1,0:T(2,128)(2,1)S(1)}, bf16[1,2048,2,512]{3,2,1,0:T(2,128)(2,1)}, u32[]{:S(2)}) copy-start(bf16[1,2048,2,512]{3,2,1,0:T(2,128)(2,1)} %param.18) | copy-start | bytes 12582916
  29.5 3.2 %copy-start.1 = (f32[2048,16]{0,1:T(8,128)S(1)}, f32[2048,16]{0,1:T(8,128)}, u32[]{:S(2)}) copy-start(f32[2048,16]{0,1:T(8,128)} %param.16) | copy-start | bytes 393220
  33.1 1.4 %copy-start.2 = (s32[32,8]{0,1:T(8,128)S(1)}, s32[32,8]{0,1:T(8,128)}, u32[]{:S(2)}) copy-start(s32[32,8]{0,1:T(8,128)} %param.17) | copy-start | bytes 3076

commit v3 on v2

--- a/solution.py
+++ b/solution.py
@@ -10,33 +10,91 @@
 HD = 128
 
 
-def attend(fresh_qkv, kv_cache, cache_len):
-    requests, ctx_len = kv_cache.shape[0], kv_cache.shape[1]
-    local_heads = fresh_qkv.shape[2] // HD
-    queries = fresh_qkv[:, 0].reshape(requests, local_heads, HD)
-    new_keys = fresh_qkv[:, 1].reshape(requests, local_heads, HD)
-    new_values = fresh_qkv[:, 2].reshape(requests, local_heads, HD)
-    cache_keys = kv_cache[:, :, 0].reshape(requests, ctx_len, local_heads, HD)
-    cache_values = kv_cache[:, :, 1].reshape(requests, ctx_len, local_heads, HD)
+def attend_kernel(ctx_len, lens, q_ref, k_ref, v_ref, kv, proj_hbm, out, proj, attended, scores, load_sem):
+    step = pl.program_id(0)
+    load = pltpu.make_async_copy(proj_hbm, proj, load_sem)
+
+    @pl.when(step == 0)
+    def _():
+        load.start()
+
+    f32, bf16 = jnp.float32, jnp.bfloat16
+    block, width = q_ref.shape
+    pair = 2 * HD
+    row = lax.broadcasted_iota(jnp.int32, (pair, pair), 0) // HD
+    column = lax.broadcasted_iota(jnp.int32, (pair, pair), 1) // HD
+    ones = jnp.where(row == column, 1.0, 0.0).astype(bf16)
     factor = HD ** (-0.5)
-    scores = (
-        jnp.einsum("nhd,nchd->nhc", queries, cache_keys, preferred_element_type=jnp.float32)
-        * factor
-    )
-    own_score = (
-        jnp.einsum("nhd,nhd->nh", queries, new_keys, preferred_element_type=jnp.float32) * factor
-    )
-    valid = (jnp.arange(ctx_len, dtype=jnp.int32)[None, :] < cache_len[:, None])[:, None, :]
-    masked = jnp.where(valid, scores, -jnp.inf)
-    top_score = jnp.maximum(jnp.max(masked, axis=-1), own_score)
-    expos = jnp.where(valid, jnp.exp(masked - top_score[..., None]), 0.0)
-    own_expo = jnp.exp(own_score - top_score)
-    total = jnp.sum(expos, axis=-1) + own_expo
-    weights = (expos / total[..., None]).astype(jnp.bfloat16)
-    own_weight = (own_expo / total).astype(jnp.bfloat16)
-    mixed = jnp.einsum("nhc,nchd->nhd", weights, cache_values, preferred_element_type=jnp.float32)
-    mixed = mixed + own_weight.astype(jnp.float32)[..., None] * new_values.astype(jnp.float32)
-    return mixed.astype(jnp.bfloat16).reshape(requests, local_heads * HD)
+
+    def head_sums(product):
+        high = product.astype(bf16)
+        low = (product - high.astype(f32)).astype(bf16)
+        return jnp.concatenate(
+            [
+                jnp.dot(high[:, at : at + pair], ones, preferred_element_type=f32)
+                + jnp.dot(low[:, at : at + pair], ones, preferred_element_type=f32)
+                for at in range(0, width, pair)
+            ],
+            axis=1,
+        )
+
+    queries = q_ref[...].astype(f32)
+    own_scores = head_sums(queries * k_ref[...].astype(f32)) * factor
+    new_values = v_ref[...].astype(f32)
+    for r in range(block):
+        scores[r * ctx_len : (r + 1) * ctx_len, :] = (
+            kv[r, :, 0, :].astype(f32) * queries[r : r + 1, :]
+        )
+    scores[...] = head_sums(scores[...]) * factor
+    position = lax.broadcasted_iota(jnp.int32, (ctx_len, width), 0)
+    rows = []
+    for r in range(block):
+        valid = position < lens[step * block + r]
+        own = own_scores[r : r + 1, :]
+        masked = jnp.where(valid, scores[r * ctx_len : (r + 1) * ctx_len, :], -jnp.inf)
+        top = jnp.maximum(jnp.max(masked, axis=0, keepdims=True), own)
+        expos = jnp.exp(masked - top)
+        own_expo = jnp.exp(own - top)
+        total = jnp.sum(expos, axis=0, keepdims=True) + own_expo
+        inverse = 1.0 / total
+        weights = (expos * inverse).astype(bf16).astype(f32)
+        own_weight = (own_expo * inverse).astype(bf16).astype(f32)
+        mixed = jnp.sum(weights * kv[r, :, 1, :].astype(f32), axis=0, keepdims=True)
+        rows.append(mixed + own_weight * new_values[r : r + 1, :])
+    attended[pl.ds(pl.multiple_of(step * block, block), block), :] = jnp.concatenate(rows, axis=0)
+
+    @pl.when(step == pl.num_programs(0) - 1)
+    def _():
+        load.wait()
+        out[...] = jnp.dot(attended[...].astype(bf16), proj[...], preferred_element_type=f32)
+
+
+def attend(fresh_qkv, kv_cache, cache_len, out_proj):
+    tokens, ctx_len, _, width = kv_cache.shape
+    block = 8
+    fresh = pl.BlockSpec((block, width), lambda i: (i, 0))
+    model = out_proj.shape[1]
+    return pl.pallas_call(
+        functools.partial(attend_kernel, ctx_len),
+        grid=(tokens // block,),
+        out_shape=jax.ShapeDtypeStruct((tokens, model), jnp.float32),
+        in_specs=[
+            pl.BlockSpec(memory_space=pltpu.SMEM),
+            fresh,
+            fresh,
+            fresh,
+            pl.BlockSpec((block, ctx_len, 2, width), lambda i: (i, 0, 0, 0)),
+            pl.BlockSpec(memory_space=pl.ANY),
+        ],
+        out_specs=pl.BlockSpec((tokens, model), lambda i: (0, 0)),
+        scratch_shapes=[
+            pltpu.VMEM(out_proj.shape, jnp.bfloat16),
+            pltpu.VMEM((tokens, width), jnp.float32),
+            pltpu.VMEM((block * ctx_len, width), jnp.float32),
+            pltpu.SemaphoreType.DMA,
+        ],
+        compiler_params=pltpu.CompilerParams(vmem_limit_bytes=40 * 1024 * 1024),
+    )(cache_len, fresh_qkv[:, 0], fresh_qkv[:, 1], fresh_qkv[:, 2], kv_cache, out_proj)
 
 
 def moe_kernel(
@@ -348,8 +406,7 @@
     down_proj,
 ):
     experts = lax.axis_size("req")
-    attended = attend(fresh_qkv, kv_cache, cache_len)
-    partial_value = jnp.dot(attended, out_proj, preferred_element_type=jnp.float32)
+    partial_value = attend(fresh_qkv, kv_cache, cache_len, out_proj)
     half = 64 * (-(-experts // 64))
     lanes = lax.rem(jnp.arange(2 * half, dtype=jnp.int32), half)
     named = jnp.any(expert_ids[:, :, None] == lanes[None, None, :], axis=1).astype(jnp.float32)

time: 82.3 us -> 72.1 us (0.88)
  local copies, waits for them, and re-layouts: 27.9 us -> 16.7 us
  Pallas kernels: 45.3 us -> 52.9 us
  matrix products: 5.37 us -> 0 us
  other arithmetic: 3.33 us -> 2.05 us
    slice x1 -> x0, local copies, waits for them, and re-layouts: 16.1 us -> none  [attend(): cache_values = kv_cache[:, :, 1].reshape(requests, ctx_len, local_heads, HD)]
    pallas_call x0 -> x1, Pallas kernels: none -> 7.67 us  [attend(): pl.pallas_call(functools.partial(attend_kernel, ctx_len), grid=(tokens //...]
    dot_general x3 -> x0, matrix products: 5.37 us -> none  [the longest x1 3.88 us: local(): jnp.dot(attended, out_proj, preferred_element_type=jnp.float32)]
    unnamed x14 -> x17, local copies, waits for them, and re-layouts: 1.97 us -> 6.62 us
    unnamed x2 -> x0, other arithmetic: 1.03 us -> none
    squeeze x0 -> x1, local copies, waits for them, and re-layouts: none -> 0.92 us  [attend(): fresh_qkv[:, 2]]
where the time goes in v3:
time: 72.1 us; the launch traced here: 71.8 us
  Pallas kernels  52.9 us (73%)
  local copies, waits for them, and re-layouts  16.7 us (23%)
  other arithmetic  2.05 us (3%)
    pallas_call x1, Pallas kernels, moe_call(): pl.pallas_call(functools.partial(moe_kernel, deep, plane, cores), out_sha...  45.3 us
    pallas_call x1, Pallas kernels, attend(): pl.pallas_call(functools.partial(attend_kernel, ctx_len), grid=(tokens //...  7.67 us
    unnamed x17, local copies, waits for them, and re-layouts  6.62 us
    slice x1, local copies, waits for them, and re-layouts, local(): gate_up[0, :, 1]  5.95 us
    squeeze x1, local copies, waits for them, and re-layouts, local(): gate_up[0, :, 1]  3.18 us

profile of v3, /device:TPU:0, one launch (start us, length us, event | category | flops | bytes accessed | tf_op | source)
XLA Modules:
  0.0 71.8 jit_solution(13844371851023752692)
XLA Ops:
  0.0 0.9 %slice_bitcast_fusion = (bf16[32,1024]{1,0:T(8,128)(2,1)S(1)}, bf16[32,1024]{1,0:T(8,128)(2,1)S(1)}, bf16[32,1024]{1,0:T(8,128)(2,1)S(1)}) fusion(bf16[32,3,1024]{2,0,1:T(8,128)(2,1)} %param.11), kind=kLoop, calls=%fused_computation.4 | loop fusion | bytes 393216 | tf_op jit(solution)/shard_map/squeeze | solution.py:97
  0.9 0.0 copy-start
  0.9 2.2 %copy-done = bf16[1024,2048]{1,0:T(8,128)(2,1)S(1)} copy-done((bf16[1024,2048]{1,0:T(8,128)(2,1)S(1)}, bf16[1024,2048]{1,0:T(8,128)(2,1)}, u32[]{:S(2)}) %copy-start) | copy-done | bytes 4194328
  3.1 0.0 copy-start.1
  3.1 1.9 %copy-done.1 = bf16[32,24,2,1024]{3,2,1,0:T(2,128)(2,1)S(1)} copy-done((bf16[32,24,2,1024]{3,2,1,0:T(2,128)(2,1)S(1)}, bf16[32,24,2,1024]{3,2,1,0:T(2,128)(2,1)}, u32[]{:S(2)}) %copy-start.1) | copy-done | bytes 3145752
  5.0 0.0 copy-start.3
  5.0 0.7 copy-done.3
  5.7 0.0 copy-start.4
  5.7 7.7 %shard_map.100.partial = f32[32,2048]{1,0:T(8,128)S(1)} custom-call(s32[32]{0:T(128)S(1)} %copy-done.3, bf16[32,1024]{1,0:T(8,128)(2,1)S(1)} %get-tuple-element.8.q_ref, bf16[32,1024]{1,0:T(8,128)(2,1)S(1)} %get-tuple-element.9.k_ref, bf16[32,1024]{1,0:T(8,128)(2,1)S(1)} %get-tuple-element.7.v_ref, bf16[32,24,2,1024]{3,2,1,0:T(2,128)(2,1)S(1)} %copy-done.1, ...), custom_call_target="tpu_custom_call" | custom-call | tf_op jit(solution)/shard_map/pallas_call | solution.py:77
  13.3 0.0 copy-done.4
  13.3 0.0 copy-start.2
  13.4 6.0 %fusion = (bf16[1,2048,1,512]{3,2,1,0:T(2,128)(2,1)S(1)}, bf16[1,2048,1,512]{3,2,1,0:T(2,128)(2,1)S(1)}) fusion(bf16[1,2048,2,512]{3,2,1,0:T(2,128)(2,1)S(1)} %copy-done.4), kind=kLoop, calls=%fused_computation.8 | loop fusion | bytes 8388608 | tf_op jit(solution)/shard_map/slice | solution.py:422
  19.3 0.0 copy-done.2
  19.3 0.0 copy-start.5
  19.3 3.2 %copy_bitcast_fusion = (bf16[2048,512]{1,0:T(8,128)(2,1)}, bf16[2048,512]{1,0:T(8,128)(2,1)}) fusion(bf16[1,2048,1,512]{3,2,1,0:T(2,128)(2,1)S(1)} %get-tuple-element.5, bf16[1,2048,1,512]{3,2,1,0:T(2,128)(2,1)S(1)} %get-tuple-element.6), kind=kLoop, calls=%fused_computation | loop fusion | bytes 8388608 | tf_op jit(solution)/shard_map/squeeze | solution.py:422
  22.5 0.0 copy-start.6
  22.5 0.0 copy-done.5
  22.5 0.3 copy.15
  22.9 0.1 pad.4
  22.9 1.3 %pad_maximum_fusion.router = f32[2048,128]{1,0:T(8,128)} fusion(f32[2048,64]{1,0:T(8,128)S(1)} %pad.4), kind=kLoop, calls=%fused_computation.2 | loop fusion | flops 262144 | bytes 1572864 | tf_op jit(solution)/shard_map/concatenate | solution.py:414
  24.2 0.0 copy-done.6
  24.2 0.1 copy.16
  24.3 0.1 compare_reduce_fusion
  24.4 0.6 convert_element_type.5.named
  25.1 45.3 %shard_map.101 = bf16[32,1024]{1,0:T(8,128)(2,1)} custom-call(f32[32,2048]{1,0:T(8,128)} %copy-done.2, bf16[32,2048]{1,0:T(8,128)(2,1)} %residual.1, f32[1,2048]{1,0:T(1,128)} %bitcast.13, f32[2048,128]{1,0:T(8,128)} %pad_maximum_fusion.router, f32[32,128]{1,0:T(8,128)} %convert_element_type.5.named, bf16[2048,512]{1,0:T(8,128)(2,1)} %get-tuple-element.11.gate_hbm, ...), custom_call_target="tpu_custom_call" | custom-call | tf_op jit(solution)/shard_map/pallas_call | solution.py:356
  70.4 1.5 %copy.24 = bf16[32,1024]{1,0:T(8,128)(2,1)} copy(bf16[32,1024]{1,0:T(8,128)(2,1)} %shard_map.101) | data formatting | bytes 131072
  (1 shorter events, 0.0 us)
Async XLA Ops:
  0.9 2.2 %copy-start = (bf16[1024,2048]{1,0:T(8,128)(2,1)S(1)}, bf16[1024,2048]{1,0:T(8,128)(2,1)}, u32[]{:S(2)}) copy-start(bf16[1024,2048]{1,0:T(8,128)(2,1)} %proj_hbm.1) | copy-start | bytes 12582916
  3.1 1.9 %copy-start.1 = (bf16[32,24,2,1024]{3,2,1,0:T(2,128)(2,1)S(1)}, bf16[32,24,2,1024]{3,2,1,0:T(2,128)(2,1)}, u32[]{:S(2)}) copy-start(bf16[32,24,2,1024]{3,2,1,0:T(2,128)(2,1)} %kv.1) | copy-start | bytes 9437188
  5.0 0.7 copy-start.3
  5.7 7.7 %copy-start.4 = (bf16[1,2048,2,512]{3,2,1,0:T(2,128)(2,1)S(1)}, bf16[1,2048,2,512]{3,2,1,0:T(2,128)(2,1)}, u32[]{:S(2)}) copy-start(bf16[1,2048,2,512]{3,2,1,0:T(2,128)(2,1)} %param.18) | copy-start | bytes 12582916
  13.3 6.0 %copy-start.2 = (f32[32,2048]{1,0:T(8,128)}, f32[32,2048]{1,0:T(8,128)S(1)}, u32[]{:S(2)}) copy-start(f32[32,2048]{1,0:T(8,128)S(1)} %shard_map.100.partial) | copy-start | bytes 786436
  19.3 3.2 %copy-start.5 = (f32[2048,16]{0,1:T(8,128)S(1)}, f32[2048,16]{0,1:T(8,128)}, u32[]{:S(2)}) copy-start(f32[2048,16]{0,1:T(8,128)} %param.16) | copy-start | bytes 393220
  22.5 1.7 %copy-start.6 = (s32[32,8]{0,1:T(8,128)S(1)}, s32[32,8]{0,1:T(8,128)}, u32[]{:S(2)}) copy-start(s32[32,8]{0,1:T(8,128)} %param.17) | copy-start | bytes 3076

commit v4 on v3

--- a/solution.py
+++ b/solution.py
@@ -93,7 +93,7 @@
             pltpu.VMEM((block * ctx_len, width), jnp.float32),
             pltpu.SemaphoreType.DMA,
         ],
-        compiler_params=pltpu.CompilerParams(vmem_limit_bytes=40 * 1024 * 1024),
+        compiler_params=pltpu.CompilerParams(vmem_limit_bytes=60 * 1024 * 1024),
     )(cache_len, fresh_qkv[:, 0], fresh_qkv[:, 1], fresh_qkv[:, 2], kv_cache, out_proj)
 
 
@@ -105,15 +105,15 @@
     residual,
     gain,
     router,
-    named,
-    gate_hbm,
-    up_hbm,
+    ids,
+    both_hbm,
     down_hbm,
     out,
     parts,
     hidden,
     normed,
     gathered,
+    both_w,
     gate_w,
     up_w,
     down_w,
@@ -148,7 +148,7 @@
 
     loads = [
         pltpu.make_async_copy(src, dst, load_sem.at[i])
-        for i, (src, dst) in enumerate(((gate_hbm, gate_w), (up_hbm, up_w), (down_hbm, down_w)))
+        for i, (src, dst) in enumerate(((both_hbm, both_w), (down_hbm, down_w)))
     ]
     for load in loads:
         load.start()
@@ -203,9 +203,21 @@
         precision=lax.Precision.HIGHEST,
         preferred_element_type=f32,
     )
-    half = router.shape[1] // 2
+    experts = router.shape[1]
+    half = 64 * (-(-experts // 64))
+    source = lax.broadcasted_iota(jnp.int32, (experts, 2 * half), 0)
+    target = lax.rem(lax.broadcasted_iota(jnp.int32, (experts, 2 * half), 1), half)
+    logits = jnp.dot(
+        logits,
+        jnp.where(source == target, 1.0, 0.0).astype(f32),
+        precision=lax.Precision.HIGHEST,
+        preferred_element_type=f32,
+    )
     lane = lax.broadcasted_iota(jnp.int32, logits.shape, 1)
-    chosen = named[...] > 0.0
+    lane_expert = lax.rem(lane, half)
+    chosen = ids[:, 0:1] == lane_expert
+    for k in range(1, ids.shape[1]):
+        chosen = chosen | (ids[:, k : k + 1] == lane_expert)
     top = jnp.max(jnp.where(chosen, logits, -jnp.inf), axis=1, keepdims=True)
     expos = jnp.where(chosen, jnp.exp(jnp.where(chosen, logits, top) - top), 0.0)
     total = jnp.sum(jnp.where(lane < half, expos, 0.0), axis=1, keepdims=True)
@@ -244,11 +256,27 @@
         send(mine, mine, own_send.at[i - 1], slot_recv.at[me], (level_at(i) * plane + place, core))
     spread(0)
     cross(0, 0)
+    loads[0].wait()
+
+    def split(k):
+        rows = 128
+        quarter = width // deep
+
+        def one(i, carry):
+            span = pl.ds(pl.multiple_of(k * quarter + i * rows, rows), rows)
+            gate_w[span, :] = both_w[span, 0, :]
+            up_w[span, :] = both_w[span, 1, :]
+            return carry
+
+        lax.fori_loop(0, quarter // rows, one, 0)
+
+    split(0)
     for k in range(1, deep):
         slot = level_at(deep - k) * plane + place
         arrived(gathered.at[core, slot], slot_recv.at[slot])
         spread(k)
         cross(k, 0)
+        split(k)
 
     def collect(k):
         first = level_at(deep - k) * plane
@@ -326,8 +354,7 @@
         if step < deep:
             collect(step)
             if step == 0:
-                for load in loads:
-                    load.wait()
+                loads[1].wait()
             work(step)
         if 1 <= step <= deep:
             over_plane(step - 1)
@@ -342,7 +369,7 @@
         copy.wait_send()
 
 
-def moe_call(partial, residual, gain, router, named, gate_w, up_w, down_w):
+def moe_call(partial, residual, gain, router, ids, both_w, down_w):
     shards, cores = lax.axis_size("req"), lax.axis_size("tp")
     deep = 4
     plane = shards // deep
@@ -356,13 +383,14 @@
     return pl.pallas_call(
         functools.partial(moe_kernel, deep, plane, cores),
         out_shape=jax.ShapeDtypeStruct((tokens, cols), bf16),
-        in_specs=[vmem] * 5 + [hbm] * 3,
+        in_specs=[vmem] * 5 + [hbm] * 2,
         out_specs=vmem,
         scratch_shapes=[
             pltpu.VMEM((others, tokens, width), jnp.float32),
             pltpu.VMEM((tokens, width), bf16),
             pltpu.VMEM((tokens, width), bf16),
-            pltpu.VMEM((cores, shards, tokens, cols + router.shape[1]), bf16),
+            pltpu.VMEM((cores, shards, tokens, cols + 128 * (-(-shards // 64))), bf16),
+            pltpu.VMEM((width, 2, units), bf16),
             pltpu.VMEM((width, units), bf16),
             pltpu.VMEM((width, units), bf16),
             pltpu.VMEM((units, width), bf16),
@@ -372,7 +400,7 @@
             pltpu.VMEM((deep, plane - 1, tokens, cols), bf16),
             pltpu.VMEM((deep - 1, tokens, cols), bf16),
             pltpu.VMEM((deep - 1, tokens, cols), bf16),
-            dma((3,)),
+            dma((2,)),
             dma((others,)),
             dma((others,)),
             dma((deep - 1,)),
@@ -390,7 +418,7 @@
         compiler_params=pltpu.CompilerParams(
             collective_id=0, has_side_effects=True, vmem_limit_bytes=56 * 1024 * 1024
         ),
-    )(partial, residual, gain, router, named, gate_w, up_w, down_w)
+    )(partial, residual, gain, router, ids, both_w, down_w)
 
 
 def local(
@@ -405,21 +433,14 @@
     gate_up,
     down_proj,
 ):
-    experts = lax.axis_size("req")
     partial_value = attend(fresh_qkv, kv_cache, cache_len, out_proj)
-    half = 64 * (-(-experts // 64))
-    lanes = lax.rem(jnp.arange(2 * half, dtype=jnp.int32), half)
-    named = jnp.any(expert_ids[:, :, None] == lanes[None, None, :], axis=1).astype(jnp.float32)
-    router = jnp.pad(router_weight, ((0, 0), (0, half - experts)))
-    router = jnp.concatenate([router, router], axis=1)
     return moe_call(
         partial_value,
         residual,
         norm_gain[None, :],
-        router,
-        named,
-        gate_up[0, :, 0],
-        gate_up[0, :, 1],
+        router_weight,
+        expert_ids,
+        gate_up[0],
         down_proj[0],
     )
 

time: 72.1 us -> 63.3 us (0.88)
  local copies, waits for them, and re-layouts: 16.7 us -> 5.76 us
  Pallas kernels: 52.9 us -> 57.2 us
  other arithmetic: 2.05 us -> 0 us
    slice x1 -> x0, local copies, waits for them, and re-layouts: 5.95 us -> none  [local(): gate_up[0, :, 1]]
    squeeze x1 -> x0, local copies, waits for them, and re-layouts: 3.18 us -> none  [local(): gate_up[0, :, 1]]
    pallas_call x1, Pallas kernels: 45.3 us -> 47.8 us  [moe_call(): pl.pallas_call(functools.partial(moe_kernel, deep, plane, cores), out_sha...]
    unnamed x17 -> x5, local copies, waits for them, and re-layouts: 6.62 us -> 4.19 us
    pallas_call x1, Pallas kernels: 7.67 us -> 9.37 us  [attend(): pl.pallas_call(functools.partial(attend_kernel, ctx_len), grid=(tokens //...]
    concatenate x1 -> x0, other arithmetic: 1.31 us -> none  [local(): router = jnp.concatenate([router, router], axis=1)]
where the time goes in v4:
time: 63.3 us; the launch traced here: 63 us
  Pallas kernels  57.2 us (90%)
  local copies, waits for them, and re-layouts  5.76 us (9%)
    pallas_call x1, Pallas kernels, moe_call(): pl.pallas_call(functools.partial(moe_kernel, deep, plane, cores), out_sha...  47.8 us
    pallas_call x1, Pallas kernels, attend(): pl.pallas_call(functools.partial(attend_kernel, ctx_len), grid=(tokens //...  9.37 us
    unnamed x5, local copies, waits for them, and re-layouts  4.19 us
    squeeze x1, local copies, waits for them, and re-layouts, attend(): fresh_qkv[:, 2]  1.56 us

profile of v4, /device:TPU:0, one launch (start us, length us, event | category | flops | bytes accessed | tf_op | source)
XLA Modules:
  0.0 63.0 jit_solution(2951223929963818069)
XLA Ops:
  0.0 0.0 copy-start
  0.0 1.4 %copy.12.ids = s32[32,8]{1,0:T(8,128)} copy(s32[32,8]{0,1:T(8,128)} %param.17) | data formatting | bytes 2048 | tf_op args[7]
  1.4 1.6 %slice_bitcast_fusion = (bf16[32,1024]{1,0:T(8,128)(2,1)}, bf16[32,1024]{1,0:T(8,128)(2,1)}, bf16[32,1024]{1,0:T(8,128)(2,1)}) fusion(bf16[32,3,1024]{2,0,1:T(8,128)(2,1)} %param.11), kind=kLoop, calls=%fused_computation | loop fusion | bytes 393216 | tf_op jit(solution)/shard_map/squeeze | solution.py:97
  3.0 9.4 %shard_map.100.partial = f32[32,2048]{1,0:T(8,128)} custom-call(s32[32]{0:T(128)} %lens.1, bf16[32,1024]{1,0:T(8,128)(2,1)} %get-tuple-element.6.q_ref, bf16[32,1024]{1,0:T(8,128)(2,1)} %get-tuple-element.7.k_ref, bf16[32,1024]{1,0:T(8,128)(2,1)} %get-tuple-element.5.v_ref, bf16[32,24,2,1024]{3,2,1,0:T(2,128)(2,1)} %kv.1, bf16[1024,2048]{1,0:T(8,128)(2,1)} %proj_hbm.1), custom_call_target="tpu_custom_call" | custom-call | tf_op jit(solution)/shard_map/pallas_call | solution.py:77
  12.3 0.0 copy-done
  12.4 1.3 %copy.11.router = f32[2048,16]{1,0:T(8,128)} copy(f32[2048,16]{0,1:T(8,128)S(1)} %copy-done) | data formatting | bytes 262144 | tf_op args[6]
  13.7 47.8 %shard_map.101 = bf16[32,1024]{1,0:T(8,128)(2,1)} custom-call(f32[32,2048]{1,0:T(8,128)} %shard_map.100.partial, bf16[32,2048]{1,0:T(8,128)(2,1)} %residual.1, f32[1,2048]{1,0:T(1,128)} %bitcast.11, f32[2048,16]{1,0:T(8,128)} %copy.11.router, s32[32,8]{1,0:T(8,128)} %copy.12.ids, bf16[2048,2,512]{2,1,0:T(2,128)(2,1)} %bitcast.9, bf16[512,2048]{1,0:T(8,128)(2,1)} %bitcast.10), custom_call_target="tpu_custom_call" | custom-call | tf_op jit(solution)/shard_map/pallas_call | solution.py:383
  61.5 1.5 %copy.14 = bf16[32,1024]{1,0:T(8,128)(2,1)} copy(bf16[32,1024]{1,0:T(8,128)(2,1)} %shard_map.101) | data formatting | bytes 131072
Async XLA Ops:
  0.0 12.3 %copy-start = (f32[2048,16]{0,1:T(8,128)S(1)}, f32[2048,16]{0,1:T(8,128)}, u32[]{:S(2)}) copy-start(f32[2048,16]{0,1:T(8,128)} %param.16) | copy-start | bytes 393220

commit v5 on v4

--- a/solution.py
+++ b/solution.py
@@ -197,27 +197,28 @@
     values = hidden[...].astype(f32)
     scale_inv = lax.rsqrt(jnp.mean(values * values, axis=-1, keepdims=True) + 1e-05)
     normed[...] = (values * scale_inv * gain[...]).astype(bf16)
-    logits = jnp.dot(
+    logits = lax.dot_general(
         normed[...].astype(f32),
         router[...],
+        (((1,), (1,)), ((), ())),
         precision=lax.Precision.HIGHEST,
         preferred_element_type=f32,
     )
-    experts = router.shape[1]
+    experts = router.shape[0]
     half = 64 * (-(-experts // 64))
     source = lax.broadcasted_iota(jnp.int32, (experts, 2 * half), 0)
     target = lax.rem(lax.broadcasted_iota(jnp.int32, (experts, 2 * half), 1), half)
-    logits = jnp.dot(
-        logits,
-        jnp.where(source == target, 1.0, 0.0).astype(f32),
-        precision=lax.Precision.HIGHEST,
-        preferred_element_type=f32,
+    lanes = jnp.where(source == target, 1.0, 0.0).astype(f32)
+    logits = jnp.dot(logits, lanes, precision=lax.Precision.HIGHEST, preferred_element_type=f32)
+    lane = lax.broadcasted_iota(jnp.int32, logits.shape, 1)
+    expert = lax.broadcasted_iota(jnp.int32, (experts, tokens), 0)
+    named = ids[0:1, :] == expert
+    for k in range(1, ids.shape[0]):
+        named = named | (ids[k : k + 1, :] == expert)
+    named = jnp.where(named, 1.0, 0.0).astype(f32)
+    chosen = (
+        lax.dot_general(named, lanes, (((0,), (0,)), ((), ())), preferred_element_type=f32) > 0.5
     )
-    lane = lax.broadcasted_iota(jnp.int32, logits.shape, 1)
-    lane_expert = lax.rem(lane, half)
-    chosen = ids[:, 0:1] == lane_expert
-    for k in range(1, ids.shape[1]):
-        chosen = chosen | (ids[:, k : k + 1] == lane_expert)
     top = jnp.max(jnp.where(chosen, logits, -jnp.inf), axis=1, keepdims=True)
     expos = jnp.where(chosen, jnp.exp(jnp.where(chosen, logits, top) - top), 0.0)
     total = jnp.sum(jnp.where(lane < half, expos, 0.0), axis=1, keepdims=True)
@@ -438,8 +439,8 @@
         partial_value,
         residual,
         norm_gain[None, :],
-        router_weight,
-        expert_ids,
+        router_weight.T,
+        expert_ids.T,
         gate_up[0],
         down_proj[0],
     )

time: 63.3 us -> 60.3 us (0.953)
  local copies, waits for them, and re-layouts: 5.76 us -> 3.03 us
    unnamed x5 -> x1, local copies, waits for them, and re-layouts: 4.19 us -> 1.47 us
where the time goes in v5:
time: 60.3 us; the launch traced here: 60.1 us
  Pallas kernels  57 us (95%)
  local copies, waits for them, and re-layouts  3.03 us (5%)
    pallas_call x1, Pallas kernels, moe_call(): pl.pallas_call(functools.partial(moe_kernel, deep, plane, cores), out_sha...  47.7 us
    pallas_call x1, Pallas kernels, attend(): pl.pallas_call(functools.partial(attend_kernel, ctx_len), grid=(tokens //...  9.34 us
    squeeze x1, local copies, waits for them, and re-layouts, attend(): fresh_qkv[:, 2]  1.56 us
    unnamed x1, local copies, waits for them, and re-layouts  1.47 us

profile of v5, /device:TPU:0, one launch (start us, length us, event | category | flops | bytes accessed | tf_op | source)
XLA Modules:
  0.0 60.1 jit_solution(16683405331515680262)
XLA Ops:
  0.0 1.6 %slice_bitcast_fusion = (bf16[32,1024]{1,0:T(8,128)(2,1)}, bf16[32,1024]{1,0:T(8,128)(2,1)}, bf16[32,1024]{1,0:T(8,128)(2,1)}) fusion(bf16[32,3,1024]{2,0,1:T(8,128)(2,1)} %param.11), kind=kLoop, calls=%fused_computation | loop fusion | bytes 393216 | tf_op jit(solution)/shard_map/squeeze | solution.py:97
  1.6 9.3 %shard_map.100.partial = f32[32,2048]{1,0:T(8,128)} custom-call(s32[32]{0:T(128)} %lens.1, bf16[32,1024]{1,0:T(8,128)(2,1)} %get-tuple-element.6.q_ref, bf16[32,1024]{1,0:T(8,128)(2,1)} %get-tuple-element.7.k_ref, bf16[32,1024]{1,0:T(8,128)(2,1)} %get-tuple-element.5.v_ref, bf16[32,24,2,1024]{3,2,1,0:T(2,128)(2,1)} %kv.1, bf16[1024,2048]{1,0:T(8,128)(2,1)} %proj_hbm.1), custom_call_target="tpu_custom_call" | custom-call | tf_op jit(solution)/shard_map/pallas_call | solution.py:77
  10.9 47.7 %shard_map.101 = bf16[32,1024]{1,0:T(8,128)(2,1)} custom-call(f32[32,2048]{1,0:T(8,128)} %shard_map.100.partial, bf16[32,2048]{1,0:T(8,128)(2,1)} %residual.1, f32[1,2048]{1,0:T(1,128)} %bitcast.14, f32[16,2048]{1,0:T(8,128)} %bitcast.13, s32[8,32]{1,0:T(8,128)} %bitcast.15, bf16[2048,2,512]{2,1,0:T(2,128)(2,1)} %bitcast.11, bf16[512,2048]{1,0:T(8,128)(2,1)} %bitcast.12), custom_call_target="tpu_custom_call" | custom-call | tf_op jit(solution)/shard_map/pallas_call | solution.py:384
  58.6 1.5 %copy.12 = bf16[32,1024]{1,0:T(8,128)(2,1)} copy(bf16[32,1024]{1,0:T(8,128)(2,1)} %shard_map.101) | data formatting | bytes 131072
